TPU v7x, 32 devices: a whole 2x2x4 slice. The times are simulated.
32 devices in a mesh: parts: 2 (over x), inst: 4 (over y, core), tp: 4 (over z).
Axes of the slice: x: 2, y: 2, z: 4, core: 2. Of those that a mesh axis runs over, the one named last changes fastest.
Arguments:
- queries: bfloat16 [4096, 8192], P(('parts', 'inst'), 'tp'), parts along dimension 0, may hold values from -8 to 8
- keys: bfloat16 [4096, 1024], P(('parts', 'inst'), 'tp'), parts along dimension 0, may hold values from -6 to 6
- values: bfloat16 [4096, 1024], P(('parts', 'inst'), 'tp'), parts along dimension 0, may hold values from -6 to 6
- prefix_pool_keys: bfloat16 [128, 64, 1024], P(('parts', 'inst'), None, 'tp'), parts along dimension 0, may hold values from -8 to 8
- prefix_pool_values: bfloat16 [128, 64, 1024], P(('parts', 'inst'), None, 'tp'), parts along dimension 0, may hold values from -6 to 6
- lengths: int32 [64], P(('parts', 'inst')), parts along dimension 0, may hold values from 1 to 64, 1536 in all
- targets: int32 [64, 1], P(('parts', 'inst')), parts along dimension 0, may hold values from 0 to 3; in each aligned block of 8 rows (0 to 7, 8 to 15, ...) at most 2 rows name the same one
- prefix_ids: int32 [64, 8], P(('parts', 'inst')), parts along dimension 0, may hold values from 0 to 15
- owners: int32 [64, 1], P(('parts', 'inst')), parts along dimension 0, may hold values from 0 to 3; in each aligned block of 8 rows (0 to 7, 8 to 15, ...) at most 2 rows name the same one
- out_weight: bfloat16 [8192, 4096], P('tp'), may hold values from -0.0625 to 0.0625
Outputs:
- projected: bfloat16 [64, 64, 4096], P(('parts', 'inst'), None, 'tp'), parts along dimension 0
- pages: bfloat16 [64, 2, 64, 1024], P(('parts', 'inst'), None, None, 'tp'), parts along dimension 0
- page_head_scales: bfloat16 [64, 2, 8], P(('parts', 'inst'), None, 'tp'), parts along dimension 0
There are 2 independent parts, one for each index of `parts`. A program takes and returns all parts, laid end to end along the dimension named above; an argument that names none is the same for every part. Nothing has to cross between parts.
Inputs may be any that keep to these rules, and one draw needn't show every extreme that they name: `targets`: no instance sends more than 2 of its blocks to one instance, and some instance receives exactly 2 from one instance. `owners`: no instance sends more than 2 of its pages to one instance, and some instance receives exactly 2 from one instance.
All inputs are finite; a program needn't handle non-finite values. No bound on the sum of `lengths` on one device may be relied on, other than what follows from the above.
Results may differ from a plain program's by a relative error of at most 0.0095.
Values may be sent and summed in bfloat16 or wider, within the bound.
A program may use at most 128 MiB of HBM per device.

v0:
```python
import math

import jax
import jax.numpy as jnp
from jax import lax
from jax.sharding import PartitionSpec as P

HEAD_SIZE = 128


def hadamard_table(size):
    index = jnp.arange(size, dtype=jnp.int32)
    common = jnp.bitwise_and(index[:, None], index[None, :])
    parity = jnp.zeros((size, size), jnp.int32)
    for bit_number in range(size.bit_length() - 1):
        parity = parity + jnp.bitwise_and(jnp.right_shift(common, bit_number), 1)
    return jnp.where(jnp.bitwise_and(parity, 1) == 0, 1.0, -1.0).astype(jnp.bfloat16)


def slot_matrix(route, groups, capacity):
    count = route.shape[0]
    chosen = (route[:, None] == jnp.arange(groups, dtype=jnp.int32)[None, :]).astype(jnp.int32)
    lower = (jnp.arange(count)[:, None] > jnp.arange(count)[None, :]).astype(jnp.int32)
    rank = jnp.sum(jnp.dot(lower, chosen) * chosen, axis=1)
    target_slot = route * capacity + rank
    return (target_slot[None, :] == jnp.arange(groups * capacity)[:, None]).astype(jnp.bfloat16)


def place(matrix, data):
    flat = data.reshape(data.shape[0], -1)
    moved = jnp.dot(matrix, flat, preferred_element_type=jnp.float32).astype(data.dtype)
    return moved.reshape((matrix.shape[0],) + data.shape[1:])


def attend(query_block, gathered_keys, gathered_values, length):
    blk = query_block.shape[0]
    kv_heads = gathered_keys.shape[1] // HEAD_SIZE
    head_group = query_block.shape[1] // gathered_keys.shape[1]
    query_rows = query_block.reshape(blk, kv_heads, head_group, HEAD_SIZE)
    key_row_list = gathered_keys.reshape(-1, kv_heads, HEAD_SIZE)
    value_row_list = gathered_values.reshape(-1, kv_heads, HEAD_SIZE)
    scores = jnp.einsum(
        "tkgd,skd->kgts", query_rows, key_row_list, preferred_element_type=jnp.float32
    ) / math.sqrt(HEAD_SIZE)
    ctx_len = key_row_list.shape[0]
    prefix_len = ctx_len - blk
    qpos = jnp.arange(blk, dtype=jnp.int32)[:, None]
    kpos = jnp.arange(ctx_len, dtype=jnp.int32)[None, :]
    own = kpos - prefix_len
    allowed = (kpos < prefix_len) | (own <= qpos) & (own < length)
    top = jnp.max(jnp.where(allowed, scores, jnp.float32(-1e30)), axis=-1, keepdims=True)
    expo = jnp.where(allowed, jnp.exp(scores - top), jnp.float32(0.0))
    total = jnp.sum(expo, axis=-1, keepdims=True)
    mixed = (
        jnp.einsum(
            "kgts,skd->kgtd",
            expo.astype(jnp.bfloat16),
            value_row_list,
            preferred_element_type=jnp.float32,
        )
        / total
    )
    mixed = mixed.transpose(2, 0, 1, 3).reshape(blk, -1)
    live = jnp.arange(blk, dtype=jnp.int32)[:, None] < length
    return jnp.where(live, mixed, jnp.float32(0.0)).astype(jnp.bfloat16)


def term_maker(flat_rows, out_weight):
    return lax.dot_general(
        out_weight, flat_rows, (((0,), (1,)), ((), ())), preferred_element_type=jnp.float32
    )


def on_device(
    queries,
    keys,
    values,
    prefix_pool_keys,
    prefix_pool_values,
    lengths,
    targets,
    prefix_ids,
    owners,
    out_weight,
):
    groups = lax.axis_size("inst")
    blocks = lengths.shape[0]
    block_len = prefix_pool_keys.shape[1]
    kv_width = keys.shape[1]
    capacity = max(1, (blocks + groups - 1) // groups)
    share = out_weight.shape[1] // lax.axis_size("tp")
    send_map = slot_matrix(targets[:, 0], groups, capacity)
    context_keys = jnp.concatenate(
        [
            prefix_pool_keys[prefix_ids].reshape(blocks, -1, kv_width),
            keys.reshape(blocks, block_len, kv_width),
        ],
        axis=1,
    )
    context_values = jnp.concatenate(
        [
            prefix_pool_values[prefix_ids].reshape(blocks, -1, kv_width),
            values.reshape(blocks, block_len, kv_width),
        ],
        axis=1,
    )
    send_q = place(send_map, queries.reshape(blocks, block_len, -1))
    send_k = place(send_map, context_keys)
    send_v = place(send_map, context_values)
    send_len = place(send_map, lengths.astype(jnp.bfloat16)[:, None])[:, 0]
    got_q, got_k, got_v, got_len = (
        lax.all_to_all(send_q, "inst", split_axis=0, concat_axis=0, tiled=True),
        lax.all_to_all(send_k, "inst", split_axis=0, concat_axis=0, tiled=True),
        lax.all_to_all(send_v, "inst", split_axis=0, concat_axis=0, tiled=True),
        lax.all_to_all(send_len, "inst", split_axis=0, concat_axis=0, tiled=True),
    )

    def per_slot(items):
        return attend(items[0], items[1], items[2], items[3].astype(jnp.int32))

    attn = lax.map(per_slot, (got_q, got_k, got_v, got_len))
    flat_rows = attn.reshape(-1, attn.shape[-1])
    mine = lax.psum_scatter(
        term_maker(flat_rows, out_weight).astype(jnp.bfloat16),
        "tp",
        scatter_dimension=0,
        tiled=True,
    ).astype(jnp.float32)
    projected = mine.T.reshape(attn.shape[0], block_len, share).astype(jnp.bfloat16)
    live = jnp.arange(block_len, dtype=jnp.int32)[None, :] < lengths[:, None]
    stacked_pages = jnp.stack(
        [keys.reshape(blocks, block_len, kv_width), values.reshape(blocks, block_len, kv_width)],
        axis=1,
    )
    stacked_pages = jnp.where(live[:, None, :, None], stacked_pages, jnp.zeros((), jnp.bfloat16))
    rotation_matrix = jnp.dot(
        stacked_pages.reshape(-1, HEAD_SIZE),
        hadamard_table(HEAD_SIZE),
        preferred_element_type=jnp.float32,
    ) / math.sqrt(HEAD_SIZE)
    rotation_matrix = rotation_matrix.reshape(
        blocks, 2, block_len, kv_width // HEAD_SIZE, HEAD_SIZE
    )
    peak = jnp.max(jnp.abs(rotation_matrix), axis=(2, 4))
    scale_factor = ((peak + 1e-06) / 8.0).astype(jnp.bfloat16)
    quantized_page = (
        rotation_matrix
        / lax.optimization_barrier(scale_factor).astype(jnp.float32)[:, :, None, :, None]
    ).astype(jnp.bfloat16)
    quantized_page = quantized_page.reshape(blocks, 2, block_len, kv_width)
    owner_map = slot_matrix(owners[:, 0], groups, capacity)
    pages, page_head_scales = (
        lax.all_to_all(
            place(owner_map, quantized_page), "inst", split_axis=0, concat_axis=0, tiled=True
        ),
        lax.all_to_all(
            place(owner_map, scale_factor), "inst", split_axis=0, concat_axis=0, tiled=True
        ),
    )
    return (projected, pages, page_head_scales)


def solution(mesh):
    return jax.shard_map(
        on_device,
        mesh=mesh,
        in_specs=(
            P(("parts", "inst"), "tp"),
            P(("parts", "inst"), "tp"),
            P(("parts", "inst"), "tp"),
            P(("parts", "inst"), None, "tp"),
            P(("parts", "inst"), None, "tp"),
            P(("parts", "inst")),
            P(("parts", "inst"), None),
            P(("parts", "inst"), None),
            P(("parts", "inst"), None),
            P("tp", None),
        ),
        out_specs=(
            P(("parts", "inst"), None, "tp"),
            P(("parts", "inst"), None, None, "tp"),
            P(("parts", "inst"), None, "tp"),
        ),
        check_vma=False,
    )
```

profile of v0, /device:TPU:0, one launch (start us, length us, event | category | flops | bytes accessed | tf_op | source)
XLA Modules:
  0.0 286.4 jit_solution(15554656121234813697)
XLA Ops:
  10.1 4.2 %all-to-all-start = ((bf16[4,2,1]{1,2,0:T(2,128)(2,1)}), bf16[4,2,1]{1,2,0:T(2,128)(2,1)S(1)}, u32[]{:S(2)}, u32[]{:S(2)}) async-start(bf16[4,2,1]{1,2,0:T(2,128)(2,1)} %all_to_all.31), calls=%async_computation | async-start | bytes 4096 | tf_op jit(solution)/shard_map/all_to_all | solution.py:115
  14.4 2.5 reshape_reshape.4
  17.6 2.5 copy.50
  20.1 4.6 %all-to-all-start.2 = ((bf16[8,64,2048]{2,1,0:T(8,128)(2,1)}), bf16[8,64,2048]{2,1,0:T(8,128)(2,1)}, u32[]{:S(2)}, u32[]{:S(2)}) async-start(bf16[8,64,2048]{2,1,0:T(8,128)(2,1)} %copy.50), calls=%async_computation.2 | async-start | bytes 4194304 | tf_op jit(solution)/shard_map/all_to_all | solution.py:112
  29.8 20.6 %all-to-all-done.2 = bf16[8,64,2048]{2,1,0:T(8,128)(2,1)} async-done(((bf16[8,64,2048]{2,1,0:T(8,128)(2,1)}), bf16[8,64,2048]{2,1,0:T(8,128)(2,1)}, u32[]{:S(2)}, u32[]{:S(2)}) %all-to-all-start.2) | async-done | bytes 2097184 | tf_op jit(solution)/shard_map/all_to_all | solution.py:112
  50.4 4.5 %all-to-all-start.1 = ((bf16[8,576,256]{2,1,0:T(8,128)(2,1)}), bf16[8,576,256]{2,1,0:T(8,128)(2,1)}, u32[]{:S(2)}, u32[]{:S(2)}) async-start(bf16[8,576,256]{2,1,0:T(8,128)(2,1)} %copy.49), calls=%async_computation.1 | async-start | bytes 4718592 | tf_op jit(solution)/shard_map/all_to_all | solution.py:113
  58.2 1.9 copy.51
  60.1 23.4 %all-to-all-done.1 = bf16[8,576,256]{2,1,0:T(8,128)(2,1)} async-done(((bf16[8,576,256]{2,1,0:T(8,128)(2,1)}), bf16[8,576,256]{2,1,0:T(8,128)(2,1)}, u32[]{:S(2)}, u32[]{:S(2)}) %all-to-all-start.1) | async-done | bytes 2359328 | tf_op jit(solution)/shard_map/all_to_all | solution.py:113
  83.5 3.6 %all-to-all-start.3 = ((bf16[8,576,256]{2,1,0:T(8,128)(2,1)}), bf16[8,576,256]{2,1,0:T(8,128)(2,1)S(1)}, u32[]{:S(2)}, u32[]{:S(2)}) async-start(bf16[8,576,256]{2,1,0:T(8,128)(2,1)} %copy.51), calls=%async_computation.3 | async-start | bytes 4718592 | tf_op jit(solution)/shard_map/all_to_all | solution.py:114
  87.5 28.1 %all-to-all-done.3 = bf16[8,576,256]{2,1,0:T(8,128)(2,1)S(1)} async-done(((bf16[8,576,256]{2,1,0:T(8,128)(2,1)}), bf16[8,576,256]{2,1,0:T(8,128)(2,1)S(1)}, u32[]{:S(2)}, u32[]{:S(2)}) %all-to-all-start.3) | async-done | bytes 2359328 | tf_op jit(solution)/shard_map/all_to_all | solution.py:114
  115.6 71.0 %while.12 = (s32[]{:T(128)}, bf16[8,64,2048]{2,1,0:T(8,128)(2,1)}, bf16[8]{0:T(256)(128)(2,1)S(1)}, bf16[8,576,256]{2,1,0:T(8,128)(2,1)}, bf16[8,64,2048]{2,1,0:...) while((s32[]{:T(128)}, bf16[8,64,2048]{2,1,0:T(8,128)(2,1)}, bf16[8]{0:T(256)(128)(2,1)S(1)}, ...), condition=%wide.region_4.5_spmd, body=%wide.region_1.4_spmd.sunk | while | flops 457620352 | bytes 8543723 | solution.py:121
  119.1 2.4 fusion.99
  128.0 2.4 fusion.99
  136.9 2.4 fusion.99
  145.7 2.4 fusion.99
  154.6 2.4 fusion.99
  163.5 2.4 fusion.99
  172.4 2.4 fusion.99
  181.2 2.4 fusion.99
  186.7 14.4 %fusion.35 = bf16[4096,512]{0,1:T(8,128)(2,1)} fusion(bf16[512,2048]{1,0:T(8,128)(2,1)} %bitcast.116, bf16[2048,4096]{1,0:T(8,128)(2,1)} %param.21), kind=kOutput, calls=%fused_computation.42 | convolution fusion | flops 8592031744 | bytes 23068672 | tf_op jit(solution)/shard_map/dot_general | solution.py:69
  204.4 3.2 %all-to-all-start.5 = ((bf16[8,2,2]{2,1,0:T(2,128)(2,1)}), bf16[8,2,2]{2,1,0:T(2,128)(2,1)S(1)}, u32[]{:S(2)}, u32[]{:S(2)}) async-start(bf16[8,2,2]{2,1,0:T(2,128)(2,1)} %copy.57), calls=%async_computation.6 | async-start | bytes 8192 | tf_op jit(solution)/shard_map/all_to_all | solution.py:156
  211.4 3.5 %all-to-all-start.4 = ((bf16[8,2,64,256]{3,2,1,0:T(8,128)(2,1)}), bf16[8,2,64,256]{3,2,1,0:T(8,128)(2,1)S(1)}, u32[]{:S(2)}, u32[]{:S(2)}) async-start(bf16[8,2,64,256]{3,2,1,0:T(8,128)(2,1)} %copy.56), calls=%async_computation.5 | async-start | bytes 1048576 | tf_op jit(solution)/shard_map/all_to_all | solution.py:153
  215.6 8.2 %all-to-all-done.4 = bf16[8,2,64,256]{3,2,1,0:T(8,128)(2,1)S(1)} async-done(((bf16[8,2,64,256]{3,2,1,0:T(8,128)(2,1)}), bf16[8,2,64,256]{3,2,1,0:T(8,128)(2,1)S(1)}, u32[]{:S(2)}, u32[]{:S(2)}) %all-to-all-start.4) | async-done | bytes 524320 | tf_op jit(solution)/shard_map/all_to_all | solution.py:153
  223.7 55.0 %reduce-scatter.2.cloned.1.call-done = bf16[1024,512]{0,1:T(8,128)(2,1)} async-done(((bf16[4096,512]{0,1:T(8,128)(2,1)}), bf16[1024,512]{0,1:T(8,128)(2,1)}) %reduce-scatter.2.cloned.1.call-update) | async-done | bytes 1048592 | tf_op jit(solution)/shard_map/reduce_scatter | solution.py:123
  (175 shorter events, 66.6 us)
Async XLA Ops:
  7.2 17.6 %copy-start = (bf16[16,64,256]{2,1,0:T(8,128)(2,1)S(1)}, bf16[16,64,256]{2,1,0:T(8,128)(2,1)}, u32[]{:S(2)}) copy-start(bf16[16,64,256]{2,1,0:T(8,128)(2,1)} %param.15) | copy-start | bytes 1572868
  10.1 9.9 %all-to-all-start = ((bf16[4,2,1]{1,2,0:T(2,128)(2,1)}), bf16[4,2,1]{1,2,0:T(2,128)(2,1)S(1)}, u32[]{:S(2)}, u32[]{:S(2)}) async-start(bf16[4,2,1]{1,2,0:T(2,128)(2,1)} %all_to_all.31), calls=%async_computation | async-start | bytes 4096 | tf_op jit(solution)/shard_map/all_to_all | solution.py:115
  20.1 4.6 %copy-start.7 = (s32[8,8]{1,0:T(8,128)S(1)}, s32[8,8]{1,0:T(8,128)}, u32[]{:S(2)}) copy-start(s32[8,8]{1,0:T(8,128)} %param.19) | copy-start | bytes 772
  20.1 30.4 %all-to-all-start.2 = ((bf16[8,64,2048]{2,1,0:T(8,128)(2,1)}), bf16[8,64,2048]{2,1,0:T(8,128)(2,1)}, u32[]{:S(2)}, u32[]{:S(2)}) async-start(bf16[8,64,2048]{2,1,0:T(8,128)(2,1)} %copy.50), calls=%async_computation.2 | async-start | bytes 4194304 | tf_op jit(solution)/shard_map/all_to_all | solution.py:112
  24.7 1.0 copy-start.3
  29.8 25.1 %copy-start.2 = (bf16[16,64,256]{2,1,0:T(8,128)(2,1)S(1)}, bf16[16,64,256]{2,1,0:T(8,128)(2,1)}, u32[]{:S(2)}) copy-start(bf16[16,64,256]{2,1,0:T(8,128)(2,1)} %param.16) | copy-start | bytes 1572868
  50.4 33.1 %all-to-all-start.1 = ((bf16[8,576,256]{2,1,0:T(8,128)(2,1)}), bf16[8,576,256]{2,1,0:T(8,128)(2,1)}, u32[]{:S(2)}, u32[]{:S(2)}) async-start(bf16[8,576,256]{2,1,0:T(8,128)(2,1)} %copy.49), calls=%async_computation.1 | async-start | bytes 4718592 | tf_op jit(solution)/shard_map/all_to_all | solution.py:113
  55.0 1.0 copy-start.5
  83.5 32.1 %all-to-all-start.3 = ((bf16[8,576,256]{2,1,0:T(8,128)(2,1)}), bf16[8,576,256]{2,1,0:T(8,128)(2,1)S(1)}, u32[]{:S(2)}, u32[]{:S(2)}) async-start(bf16[8,576,256]{2,1,0:T(8,128)(2,1)} %copy.51), calls=%async_computation.3 | async-start | bytes 4718592 | tf_op jit(solution)/shard_map/all_to_all | solution.py:114
  87.2 191.6 %reduce-scatter.2.cloned.1.call-start = ((), (), s32[]{:S(2)}) async-start(), calls=%async_computation.7 | async-start | bytes 5242880 | tf_op jit(solution)/shard_map/reduce_scatter | solution.py:123
  201.1 0.7 copy-start.8
  201.1 1.0 copy-start.4
  201.1 1.0 copy-start.6
  202.1 1.3 copy-start.9
  204.4 7.0 %all-to-all-start.5 = ((bf16[8,2,2]{2,1,0:T(2,128)(2,1)}), bf16[8,2,2]{2,1,0:T(2,128)(2,1)S(1)}, u32[]{:S(2)}, u32[]{:S(2)}) async-start(bf16[8,2,2]{2,1,0:T(2,128)(2,1)} %copy.57), calls=%async_computation.6 | async-start | bytes 8192 | tf_op jit(solution)/shard_map/all_to_all | solution.py:156
  208.3 71.2 %copy-start.1 = (bf16[16,64,256]{2,1,0:T(8,128)(2,1)S(1)}, bf16[16,64,256]{2,1,0:T(8,128)(2,1)}, u32[]{:S(2)}) copy-start(bf16[16,64,256]{2,1,0:T(8,128)(2,1)} %param.15) | copy-start | bytes 1572868
  211.4 12.3 %all-to-all-start.4 = ((bf16[8,2,64,256]{3,2,1,0:T(8,128)(2,1)}), bf16[8,2,64,256]{3,2,1,0:T(8,128)(2,1)S(1)}, u32[]{:S(2)}, u32[]{:S(2)}) async-start(bf16[8,2,64,256]{3,2,1,0:T(8,128)(2,1)} %copy.56), calls=%async_computation.5 | async-start | bytes 1048576 | tf_op jit(solution)/shard_map/all_to_all | solution.py:153
Sparse Core Ops, SparseCore 0:
  201.2 77.4 reduce-scatter.1
where the time goes:
time: 288 us; the launch traced here: 286 us
  waiting for transfers between devices  137 us (48%)
  matrix products  52.9 us (18%)
  local copies, waits for them, and re-layouts  43.9 us (15%)
  starting transfers between devices  23.9 us (8%)
  between operations  14.3 us (5%)
  other arithmetic  8.4 us (3%)
  loops' own time  5.86 us (2%)
    reduce_scatter x1, waiting for transfers between devices, on_device(): lax.psum_scatter(term_maker(flat_rows, out_weight).astype(jnp.bfloat16),...  55 us
    all_to_all x1, waiting for transfers between devices, on_device(): lax.all_to_all(send_v, 'inst', split_axis=0, concat_axis=0, tiled=True)  28.1 us
    all_to_all x1, waiting for transfers between devices, on_device(): lax.all_to_all(send_k, 'inst', split_axis=0, concat_axis=0, tiled=True)  23.4 us
    all_to_all x1, waiting for transfers between devices, on_device(): lax.all_to_all(send_q, 'inst', split_axis=0, concat_axis=0, tiled=True)  20.6 us
    sub x8, matrix products, attend(): expo = jnp.where(allowed, jnp.exp(scores - top), jnp.float32(0.0))  19.3 us
    dot_general x8, matrix products, attend(): jnp.einsum('kgts,skd->kgtd', expo.astype(jnp.bfloat16), value_row_list, p...  14.4 us
    dot_general x1, matrix products, term_maker(): lax.dot_general(out_weight, flat_rows, (((0,), (1,)), ((), ())), preferre...  14.4 us
    dynamic_slice x16, local copies, waits for them, and re-layouts, on_device(): attn = lax.map(per_slot, (got_q, got_k, got_v, got_len))  12.7 us
  transfers between devices with their start and end apart: 7, of which 6 were waited for; matrix products, arithmetic and copies ran while one was open for 7% of the time, Pallas kernels for 0%

commit v1 on v0

v1 whole, which is shorter than its diff:
```python
import functools
import math

import jax
import jax.numpy as jnp
from jax import lax
from jax.experimental import pallas as pl
from jax.experimental.pallas import tpu as pltpu
from jax.sharding import PartitionSpec as P

HEAD_SIZE = 128
MESH = pl.DeviceIdType.MESH


def hadamard_table(size):
    row = lax.broadcasted_iota(jnp.int32, (size, size), 0)
    col = lax.broadcasted_iota(jnp.int32, (size, size), 1)
    common = jnp.bitwise_and(row, col)
    parity = jnp.zeros((size, size), jnp.int32)
    for bit_number in range(size.bit_length() - 1):
        parity = parity + jnp.bitwise_and(jnp.right_shift(common, bit_number), 1)
    return jnp.where(jnp.bitwise_and(parity, 1) == 0, 1.0, -1.0).astype(jnp.bfloat16)


def block_of(route_ref, blocks, group, rank):
    seen, found, valid = jnp.int32(0), jnp.int32(0), jnp.int32(0)
    for b in range(blocks):
        hit = (route_ref[b, 0] == group).astype(jnp.int32)
        take = hit * (seen == rank).astype(jnp.int32)
        found = found + take * b
        valid = valid + take
        seen = seen + hit
    return found, valid


def attend(q_ref, k_ref, v_ref, pk_ref, pv_ref, ids_ref, block, length, attn_ref, row):
    block_len = q_ref.shape[1]
    kv_heads = k_ref.shape[2] // HEAD_SIZE
    group = q_ref.shape[2] // k_ref.shape[2]
    attended = ids_ref.shape[1]
    rate = math.log2(math.e) / math.sqrt(HEAD_SIZE)
    rows = group * block_len
    nt = (((1,), (1,)), ((), ()))
    token = lax.rem(lax.broadcasted_iota(jnp.int32, (rows, block_len), 0), block_len)
    place = lax.broadcasted_iota(jnp.int32, (rows, block_len), 1)
    allowed = (place <= token) & (place < length)
    live = lax.broadcasted_iota(jnp.int32, (block_len, HEAD_SIZE), 0) < length
    ids = [ids_ref[block, a] for a in range(attended)]
    for h in range(kv_heads):
        lanes = slice(h * HEAD_SIZE, (h + 1) * HEAD_SIZE)
        base = h * group * HEAD_SIZE
        q = jnp.concatenate(
            [q_ref[block, :, base + g * HEAD_SIZE : base + (g + 1) * HEAD_SIZE] for g in range(group)], axis=0
        )
        prefix_k = jnp.concatenate([pk_ref[i, :, lanes] for i in ids], axis=0)
        prefix_v = jnp.concatenate([pv_ref[i, :, lanes] for i in ids], axis=0)
        s0 = lax.dot_general(q, prefix_k, nt, preferred_element_type=jnp.float32)
        s1 = lax.dot_general(q, k_ref[block, :, lanes], nt, preferred_element_type=jnp.float32)
        s1 = jnp.where(allowed, s1, jnp.float32(-1e30))
        top = jnp.maximum(
            jnp.max(s0, axis=1, keepdims=True), jnp.max(s1, axis=1, keepdims=True)
        )
        p0 = jnp.exp2((s0 - top) * rate).astype(jnp.bfloat16)
        p1 = jnp.where(allowed, jnp.exp2((s1 - top) * rate), 0.0).astype(jnp.bfloat16)
        v0 = jnp.concatenate([prefix_v, jnp.ones_like(prefix_v)], axis=1)
        own_v = v_ref[block, :, lanes]
        v1 = jnp.concatenate([own_v, jnp.ones_like(own_v)], axis=1)
        mixed = jnp.dot(p0, v0, preferred_element_type=jnp.float32) + jnp.dot(
            p1, v1, preferred_element_type=jnp.float32
        )
        mixed = mixed[:, :HEAD_SIZE] / mixed[:, HEAD_SIZE:]
        for g in range(group):
            part = mixed[g * block_len : (g + 1) * block_len]
            attn_ref[row, :, base + g * HEAD_SIZE : base + (g + 1) * HEAD_SIZE] = jnp.where(
                live, part, 0.0
            ).astype(jnp.bfloat16)


def make_page(k_ref, v_ref, block, length, valid, table, page_ref, scale_ref, at, row):
    block_len = k_ref.shape[1]
    kv_heads = k_ref.shape[2] // HEAD_SIZE
    live = lax.broadcasted_iota(jnp.int32, (block_len, HEAD_SIZE), 0) < length
    tile_row = lax.broadcasted_iota(jnp.int32, (8, HEAD_SIZE), 0)
    tile_lane = lax.broadcasted_iota(jnp.int32, (8, HEAD_SIZE), 1)
    tile = jnp.zeros((8, HEAD_SIZE), jnp.float32)
    for which, ref in enumerate((k_ref, v_ref)):
        for h in range(kv_heads):
            lanes = slice(h * HEAD_SIZE, (h + 1) * HEAD_SIZE)
            data = jnp.where(live, ref[block, :, lanes].astype(jnp.float32), 0.0).astype(jnp.bfloat16)
            rot = jnp.dot(data, table, preferred_element_type=jnp.float32) / math.sqrt(HEAD_SIZE)
            peak = jnp.max(jnp.max(jnp.abs(rot), axis=1, keepdims=True), axis=0, keepdims=True)
            scale = ((peak + 1e-06) / 8.0).astype(jnp.bfloat16).astype(jnp.float32)
            page_ref[at, row, which * block_len : (which + 1) * block_len, lanes] = (
                rot / scale
            ).astype(jnp.bfloat16)
            tile = jnp.where((tile_row == which) & (tile_lane == h), scale, tile)
    scale_ref[at, row] = tile * valid.astype(jnp.float32)


def kernel(
    groups, tps, capacity,
    q_ref, k_ref, v_ref, pk_ref, pv_ref, len_ref, tgt_ref, ids_ref, own_ref, w_ref,
    proj_ref, page_ref, scale_ref,
    w_buf, attn, send, recv, final, page_buf, scale_buf,
    w_sem, send_sem, recv_sem, ship_send, ship_recv, page_send, page_recv, scale_send, scale_recv, local_sem,
):
    part, inst, me = lax.axis_index("parts"), lax.axis_index("inst"), lax.axis_index("tp")
    blocks, block_len = q_ref.shape[0], q_ref.shape[1]
    share = w_buf.shape[2]
    last = tps - 1
    far = last - me

    def dest_at(p):
        right = p < far
        return jnp.where(right, last - p, jnp.where(p < last, p - far, me))

    def w_copy(p):
        j = dest_at(p)
        columns = pl.ds(pl.multiple_of(j * share, share), share)
        return pltpu.make_async_copy(w_ref.at[:, columns], w_buf.at[j], w_sem.at[p])

    for p in range(tps):
        w_copy(p).start()

    barrier = pltpu.get_barrier_semaphore()
    for d in range(1, groups):
        other = lax.rem(inst + d, groups)
        pl.semaphore_signal(barrier, inc=1, device_id=(part, other, me), device_id_type=MESH)

    @pl.when(me > 0)
    def _():
        pl.semaphore_signal(barrier, inc=1, device_id=(part, inst, me - 1), device_id_type=MESH)

    @pl.when(me < last)
    def _():
        pl.semaphore_signal(barrier, inc=1, device_id=(part, inst, me + 1), device_id_type=MESH)

    def target(i):
        return lax.rem(inst + 1 + i, groups)

    def source(i):
        return lax.rem(inst + groups - 1 - i, groups)

    table = hadamard_table(HEAD_SIZE)

    def page_step(n, carry):
        i, r = n // capacity, n % capacity
        b, valid = block_of(own_ref, blocks, target(i), r)
        length = len_ref[b] * valid
        make_page(k_ref, v_ref, b, length, valid, table, page_buf, scale_buf, i, r)
        return carry

    lax.fori_loop(0, groups * capacity, page_step, 0)

    neighbours = (me > 0).astype(jnp.int32) + (me < last).astype(jnp.int32)
    pl.semaphore_wait(barrier, groups - 1 + neighbours)

    def page_copies(i, home):
        to = (part, target(i), me)
        slots = pl.ds(home * capacity, capacity)
        return (
            pltpu.make_async_remote_copy(
                src_ref=page_buf.at[i], dst_ref=page_ref.at[slots],
                send_sem=page_send.at[i], recv_sem=page_recv.at[i], device_id=to, device_id_type=MESH,
            ),
            pltpu.make_async_remote_copy(
                src_ref=scale_buf.at[i], dst_ref=scale_ref.at[slots],
                send_sem=scale_send.at[i], recv_sem=scale_recv.at[i], device_id=to, device_id_type=MESH,
            ),
        )

    def ship_copy(i, home):
        rows = pl.ds(pl.multiple_of(home * capacity * block_len, capacity * block_len), capacity * block_len)
        return pltpu.make_async_remote_copy(
            src_ref=final.at[i], dst_ref=proj_ref.at[rows],
            send_sem=ship_send.at[i], recv_sem=ship_recv.at[i],
            device_id=(part, target(i), me), device_id_type=MESH,
        )

    own = groups - 1
    own_slots = pl.ds(inst * capacity, capacity)
    own_rows = pl.ds(pl.multiple_of(inst * capacity * block_len, capacity * block_len), capacity * block_len)
    local_copies = (
        pltpu.make_async_copy(page_buf.at[own], page_ref.at[own_slots], local_sem.at[0]),
        pltpu.make_async_copy(scale_buf.at[own], scale_ref.at[own_slots], local_sem.at[1]),
        pltpu.make_async_copy(final.at[own], proj_ref.at[own_rows], local_sem.at[2]),
    )
    for i in range(groups - 1):
        for copy in page_copies(i, inst):
            copy.start()
    local_copies[0].start()
    local_copies[1].start()

    def sum_copy(i, j):
        towards = jnp.where(j > me, me + 1, me - 1)
        slot = jnp.where((j < me) & (j == towards), tps, j)
        return pltpu.make_async_remote_copy(
            src_ref=send.at[i, j], dst_ref=recv.at[i, slot],
            send_sem=send_sem.at[i, j], recv_sem=recv_sem.at[i, slot],
            device_id=(part, inst, towards), device_id_type=MESH,
        )

    def arrived(i, slot):
        pltpu.make_async_copy(recv.at[i, slot], recv.at[i, slot], recv_sem.at[i, slot]).wait()

    def has_upstream(j):
        return ((j > me) & (me > 0)) | ((j < me) & (me < last))

    def compute(i):
        def one(r, carry):
            b, valid = block_of(tgt_ref, blocks, target(i), r)
            attend(q_ref, k_ref, v_ref, pk_ref, pv_ref, ids_ref, b, len_ref[b] * valid, attn, r)
            return carry

        lax.fori_loop(0, capacity, one, 0)
        wide = 256 if share % 256 == 0 else share

        def term(p, carry):
            j = dest_at(p)

            @pl.when(i == 0)
            def _():
                w_copy(p).wait()

            def columns(c, inner):
                lanes = pl.ds(pl.multiple_of(c * wide, wide), wide)
                rows = attn[...].reshape(capacity * block_len, attn.shape[2])
                send[i, j, :, lanes] = jnp.dot(
                    rows, w_buf[j, :, lanes], preferred_element_type=jnp.float32
                ).astype(jnp.bfloat16)
                return inner

            lax.fori_loop(0, share // wide, columns, 0)

            @pl.when((p < last) & jnp.logical_not(has_upstream(j)))
            def _():
                sum_copy(i, j).start()

            return carry

        lax.fori_loop(0, tps, term, 0)

    def forward(i):
        def one(p, carry):
            j = dest_at(p)

            @pl.when(has_upstream(j))
            def _():
                arrived(i, j)
                send[i, j] = (send[i, j].astype(jnp.float32) + recv[i, j].astype(jnp.float32)).astype(jnp.bfloat16)
                sum_copy(i, j).start()

            return carry

        lax.fori_loop(0, last, one, 0)

    def finish(i):
        final[i] = send[i, me]

        @pl.when((me > 0) & (me < last))
        def _():
            arrived(i, me)
            arrived(i, tps)
            final[i] = (
                send[i, me].astype(jnp.float32)
                + recv[i, me].astype(jnp.float32)
                + recv[i, tps].astype(jnp.float32)
            ).astype(jnp.bfloat16)

        @pl.when((me > 0) & (me == last))
        def _():
            arrived(i, me)
            final[i] = (send[i, me].astype(jnp.float32) + recv[i, me].astype(jnp.float32)).astype(jnp.bfloat16)

        @pl.when((me == 0) & (me < last))
        def _():
            arrived(i, tps)
            final[i] = (send[i, me].astype(jnp.float32) + recv[i, tps].astype(jnp.float32)).astype(jnp.bfloat16)

        @pl.when(i < own)
        def _():
            ship_copy(i, inst).start()

    def step(i, carry):
        @pl.when(i < groups)
        def _():
            compute(i)

        @pl.when(i > 0)
        def _():
            forward(i - 1)

        @pl.when(i > 1)
        def _():
            finish(i - 2)

        return carry

    lax.fori_loop(0, groups + 1, step, 0)
    finish(own)
    local_copies[2].start()

    def drain(i, carry):
        def one(p, inner):
            sum_copy(i, dest_at(p)).wait_send()
            return inner

        return lax.fori_loop(0, last, one, carry)

    lax.fori_loop(0, groups, drain, 0)
    for i in range(groups - 1):
        ship_copy(i, inst).wait_send()
        for copy in page_copies(i, inst):
            copy.wait_send()
        ship_copy(i, source(i)).wait_recv()
        for copy in page_copies(i, source(i)):
            copy.wait_recv()
    for copy in local_copies:
        copy.wait()


def on_device(
    queries, keys, values, prefix_pool_keys, prefix_pool_values,
    lengths, targets, prefix_ids, owners, out_weight,
):
    groups, tps = lax.axis_size("inst"), lax.axis_size("tp")
    blocks, block_len = lengths.shape[0], prefix_pool_keys.shape[1]
    kv_width = keys.shape[1]
    kv_heads = kv_width // HEAD_SIZE
    capacity = max(1, (blocks + groups - 1) // groups)
    depth, dout = out_weight.shape
    share = dout // tps
    slots = groups * capacity
    rows = capacity * block_len
    vmem = pl.BlockSpec(memory_space=pltpu.VMEM)
    smem = pl.BlockSpec(memory_space=pltpu.SMEM)
    anywhere = pl.BlockSpec(memory_space=pl.ANY)
    dma = pltpu.SemaphoreType.DMA
    bf16 = jnp.bfloat16
    proj, pages, scales = pl.pallas_call(
        functools.partial(kernel, groups, tps, capacity),
        out_shape=(
            jax.ShapeDtypeStruct((slots * block_len, share), bf16),
            jax.ShapeDtypeStruct((slots, 2 * block_len, kv_width), bf16),
            jax.ShapeDtypeStruct((slots, 8, HEAD_SIZE), jnp.float32),
        ),
        in_specs=[vmem] * 5 + [smem] * 4 + [anywhere],
        out_specs=(anywhere,) * 3,
        scratch_shapes=[
            pltpu.VMEM((tps, depth, share), bf16),
            pltpu.VMEM((capacity, block_len, depth), bf16),
            pltpu.VMEM((groups, tps, rows, share), bf16),
            pltpu.VMEM((groups, tps + 1, rows, share), bf16),
            pltpu.VMEM((groups, rows, share), bf16),
            pltpu.VMEM((groups, capacity, 2 * block_len, kv_width), bf16),
            pltpu.VMEM((groups, capacity, 8, HEAD_SIZE), jnp.float32),
            dma((tps,)),
            dma((groups, tps)),
            dma((groups, tps + 1)),
            dma((groups,)), dma((groups,)),
            dma((groups,)), dma((groups,)),
            dma((groups,)), dma((groups,)),
            dma((3,)),
        ],
        compiler_params=pltpu.CompilerParams(
            collective_id=0, has_side_effects=True, vmem_limit_bytes=56 * 2**20
        ),
        cost_estimate=pl.CostEstimate(
            flops=2 * blocks * block_len * depth * (dout + 2 * 576),
            bytes_accessed=2 * depth * dout, transcendentals=0,
        ),
    )(
        queries.reshape(blocks, block_len, -1),
        keys.reshape(blocks, block_len, kv_width),
        values.reshape(blocks, block_len, kv_width),
        prefix_pool_keys, prefix_pool_values, lengths, targets, prefix_ids, owners, out_weight,
    )
    return (
        proj.reshape(slots, block_len, share),
        pages.reshape(slots, 2, block_len, kv_width),
        scales[:, :2, :kv_heads].astype(bf16),
    )


def solution(mesh):
    return jax.shard_map(
        on_device,
        mesh=mesh,
        in_specs=(
            P(("parts", "inst"), "tp"),
            P(("parts", "inst"), "tp"),
            P(("parts", "inst"), "tp"),
            P(("parts", "inst"), None, "tp"),
            P(("parts", "inst"), None, "tp"),
            P(("parts", "inst")),
            P(("parts", "inst"), None),
            P(("parts", "inst"), None),
            P(("parts", "inst"), None),
            P("tp", None),
        ),
        out_specs=(
            P(("parts", "inst"), None, "tp"),
            P(("parts", "inst"), None, None, "tp"),
            P(("parts", "inst"), None, "tp"),
        ),
        check_vma=False,
    )
```

time: 288 us -> 107 us (0.37)
  waiting for transfers between devices: 137 us -> 0 us
  Pallas kernels: 0 us -> 98.1 us
  matrix products: 52.9 us -> 0 us
  local copies, waits for them, and re-layouts: 43.9 us -> 8.2 us
  starting transfers between devices: 23.9 us -> 0 us
  between operations: 14.3 us -> 0.64 us
  other arithmetic: 8.4 us -> 0 us
  loops' own time: 5.86 us -> 0 us
    pallas_call x0 -> x1, Pallas kernels: none -> 98.1 us  [on_device(): pl.pallas_call(functools.partial(kernel, groups, tps, capacity), out_shap...]
    all_to_all x6 -> x0, waiting for transfers between devices: 82.2 us -> none  [the longest x1 28.1 us: on_device(): lax.all_to_all(send_v, 'inst', split_axis=0, concat_axis=0, tiled=True)]
    reduce_scatter x1 -> x0, waiting for transfers between devices: 55 us -> none  [on_device(): lax.psum_scatter(term_maker(flat_rows, out_weight).astype(jnp.bfloat16),...]
    dot_general x18 -> x0, matrix products: 33.6 us -> none  [the longest x8 14.4 us: attend(): jnp.einsum('kgts,skd->kgtd', expo.astype(jnp.bfloat16), value_row_list, p...]
    all_to_all x6 -> x0, starting transfers between devices: 23.6 us -> none  [the longest x1 4.58 us: on_device(): lax.all_to_all(send_q, 'inst', split_axis=0, concat_axis=0, tiled=True)]
    sub x8 -> x0, matrix products: 19.3 us -> none  [attend(): expo = jnp.where(allowed, jnp.exp(scores - top), jnp.float32(0.0))]
    dynamic_slice x16 -> x0, local copies, waits for them, and re-layouts: 12.7 us -> none  [on_device(): attn = lax.map(per_slot, (got_q, got_k, got_v, got_len))]
    reshape x30 -> x0, local copies, waits for them, and re-layouts: 10.2 us -> none  [the longest x5 7.93 us: place(): return moved.reshape((matrix.shape[0],) + data.shape[1:])]
  transfers between devices with their start and end apart: 7 -> 0, of which waited for: 6 -> 0; matrix products, arithmetic and copies ran while one was open for 7% -> 0% of each run, Pallas kernels for 0% -> 0%
where the time goes in v1:
time: 107 us
  Pallas kernels  98.1 us (92%)
  local copies, waits for them, and re-layouts  8.2 us (8%)
    pallas_call x1, Pallas kernels, on_device(): pl.pallas_call(functools.partial(kernel, groups, tps, capacity), out_shap...  98.1 us
    unnamed x5, local copies, waits for them, and re-layouts  7.44 us

profile of v1, /device:TPU:0, one launch (start us, length us, event | category | flops | bytes accessed | tf_op | source)
XLA Modules:
  0.0 107.0 jit_solution(6246910648854886613)
XLA Ops:
  0.6 1.3 %copy.13.tgt_ref = s32[8,1]{1,0:T(8,128)} copy(s32[8,1]{0,1:T(1,128)} %param.16) | data formatting | bytes 64 | tf_op args[6]
  2.0 1.3 %copy.14.own_ref = s32[8,1]{1,0:T(8,128)} copy(s32[8,1]{0,1:T(1,128)} %param.18) | data formatting | bytes 64 | tf_op args[8]
  3.3 98.1 %shard_map.121 = (bf16[512,1024]{1,0:T(8,128)(2,1)}, bf16[8,128,256]{2,1,0:T(8,128)(2,1)}, f32[8,8,128]{2,1,0:T(8,128)}) custom-call(bf16[8,64,2048]{2,1,0:T(8,128)(2,1)} %bitcast.7, bf16[8,64,256]{2,1,0:T(8,128)(2,1)} %bitcast.8, bf16[8,64,256]{2,1,0:T(8,128)(2,1)} %bitcast.9, bf16[16,64,256]{2,1,0:T(8,128)(2,1)} %pk_ref.1, bf16[16,64,256]{2,1,0:T(8,128)(2,1)} %pv_ref.1, ...), custom_call_target="tpu_custom_call" | custom-call | flops 11005853696 | bytes 16777216 | tf_op jit(solution)/shard_map/pallas_call | solution.py:340
  101.4 0.8 slice.7
  102.2 0.7 copy.15
  102.8 2.3 %copy.18 = bf16[8,64,1024]{2,1,0:T(8,128)(2,1)} copy(bf16[8,64,1024]{2,1,0:T(8,128)(2,1)} %bitcast.5) | data formatting | bytes 2097152
  105.1 1.9 %copy.19 = bf16[8,2,64,256]{3,2,1,0:T(8,128)(2,1)} copy(bf16[8,2,64,256]{3,2,1,0:T(8,128)(2,1)} %bitcast.6) | data formatting | bytes 1048576

commit v2 on v1

--- a/solution.py
+++ b/solution.py
@@ -10,6 +10,8 @@
 
 HEAD_SIZE = 128
 MESH = pl.DeviceIdType.MESH
+DEPTH = 2
+PIECES = 4
 
 
 def hadamard_table(size):
@@ -25,7 +27,7 @@
 def block_of(route_ref, blocks, group, rank):
     seen, found, valid = jnp.int32(0), jnp.int32(0), jnp.int32(0)
     for b in range(blocks):
-        hit = (route_ref[b, 0] == group).astype(jnp.int32)
+        hit = (route_ref[b] == group).astype(jnp.int32)
         take = hit * (seen == rank).astype(jnp.int32)
         found = found + take * b
         valid = valid + take
@@ -81,7 +83,6 @@
     kv_heads = k_ref.shape[2] // HEAD_SIZE
     live = lax.broadcasted_iota(jnp.int32, (block_len, HEAD_SIZE), 0) < length
     tile_row = lax.broadcasted_iota(jnp.int32, (8, HEAD_SIZE), 0)
-    tile_lane = lax.broadcasted_iota(jnp.int32, (8, HEAD_SIZE), 1)
     tile = jnp.zeros((8, HEAD_SIZE), jnp.float32)
     for which, ref in enumerate((k_ref, v_ref)):
         for h in range(kv_heads):
@@ -93,7 +94,7 @@
             page_ref[at, row, which * block_len : (which + 1) * block_len, lanes] = (
                 rot / scale
             ).astype(jnp.bfloat16)
-            tile = jnp.where((tile_row == which) & (tile_lane == h), scale, tile)
+            tile = jnp.where(tile_row == which * kv_heads + h, scale, tile)
     scale_ref[at, row] = tile * valid.astype(jnp.float32)
 
 
@@ -150,10 +151,6 @@
         make_page(k_ref, v_ref, b, length, valid, table, page_buf, scale_buf, i, r)
         return carry
 
-    lax.fori_loop(0, groups * capacity, page_step, 0)
-
-    neighbours = (me > 0).astype(jnp.int32) + (me < last).astype(jnp.int32)
-    pl.semaphore_wait(barrier, groups - 1 + neighbours)
 
     def page_copies(i, home):
         to = (part, target(i), me)
@@ -185,11 +182,14 @@
         pltpu.make_async_copy(scale_buf.at[own], scale_ref.at[own_slots], local_sem.at[1]),
         pltpu.make_async_copy(final.at[own], proj_ref.at[own_rows], local_sem.at[2]),
     )
-    for i in range(groups - 1):
-        for copy in page_copies(i, inst):
-            copy.start()
-    local_copies[0].start()
-    local_copies[1].start()
+
+    def send_pages():
+        lax.fori_loop(0, groups * capacity, page_step, 0)
+        for i in range(groups - 1):
+            for copy in page_copies(i, inst):
+                copy.start()
+        local_copies[0].start()
+        local_copies[1].start()
 
     def sum_copy(i, j):
         towards = jnp.where(j > me, me + 1, me - 1)
@@ -213,6 +213,12 @@
             return carry
 
         lax.fori_loop(0, capacity, one, 0)
+
+        @pl.when(i == 0)
+        def _():
+            neighbours = (me > 0).astype(jnp.int32) + (me < last).astype(jnp.int32)
+            pl.semaphore_wait(barrier, groups - 1 + neighbours)
+
         wide = 256 if share % 256 == 0 else share
 
         def term(p, carry):
@@ -234,11 +240,22 @@
 
             @pl.when((p < last) & jnp.logical_not(has_upstream(j)))
             def _():
+                number = i * last + p
+
+                @pl.when(number >= DEPTH)
+                def _():
+                    before = number - DEPTH
+                    sum_copy(before // last, dest_at(before % last)).wait_send()
+
                 sum_copy(i, j).start()
 
             return carry
 
         lax.fori_loop(0, tps, term, 0)
+
+        @pl.when(i == 0)
+        def _():
+            send_pages()
 
     def forward(i):
         def one(p, carry):
@@ -302,7 +319,10 @@
 
     def drain(i, carry):
         def one(p, inner):
-            sum_copy(i, dest_at(p)).wait_send()
+            @pl.when(((me > 0) & (me < last)) | (i * last + p >= groups * last - DEPTH))
+            def _():
+                sum_copy(i, dest_at(p)).wait_send()
+
             return inner
 
         return lax.fori_loop(0, last, one, carry)
@@ -317,6 +337,18 @@
             copy.wait_recv()
     for copy in local_copies:
         copy.wait()
+
+
+def deliver(proj_ref, page_ref, scale_ref, proj_out, page_out, scale_out):
+    proj_out[...] = proj_ref[...]
+    page_out[...] = page_ref[...]
+    slots, kv_heads = scale_ref.shape[0], scale_out.shape[1]
+    lane = lax.broadcasted_iota(jnp.int32, (8, HEAD_SIZE), 1)
+    table = jnp.zeros((8, HEAD_SIZE), jnp.float32)
+    for s in range(slots):
+        table = jnp.where(lane == s, scale_ref[s], table)
+    for which in range(2):
+        scale_out[which] = table[which * kv_heads : (which + 1) * kv_heads, :slots].astype(scale_out.dtype)
 
 
 def on_device(
@@ -373,12 +405,28 @@
         queries.reshape(blocks, block_len, -1),
         keys.reshape(blocks, block_len, kv_width),
         values.reshape(blocks, block_len, kv_width),
-        prefix_pool_keys, prefix_pool_values, lengths, targets, prefix_ids, owners, out_weight,
+        prefix_pool_keys, prefix_pool_values, lengths, targets.reshape(blocks), prefix_ids,
+        owners.reshape(blocks), out_weight,
     )
+    proj_spec = pl.BlockSpec((slots * block_len // PIECES, share), lambda n: (n, 0))
+    page_spec = pl.BlockSpec((slots // PIECES, 2 * block_len, kv_width), lambda n: (n, 0, 0))
+    scale_spec = pl.BlockSpec((slots, 8, HEAD_SIZE), lambda n: (0, 0, 0))
+    table_spec = pl.BlockSpec((2, kv_heads, slots), lambda n: (0, 0, 0))
+    proj, pages, scales = pl.pallas_call(
+        deliver,
+        out_shape=(
+            jax.ShapeDtypeStruct(proj.shape, bf16),
+            jax.ShapeDtypeStruct(pages.shape, bf16),
+            jax.ShapeDtypeStruct((2, kv_heads, slots), bf16),
+        ),
+        grid=(PIECES,),
+        in_specs=[proj_spec, page_spec, scale_spec],
+        out_specs=(proj_spec, page_spec, table_spec),
+    )(proj, pages, scales)
     return (
         proj.reshape(slots, block_len, share),
         pages.reshape(slots, 2, block_len, kv_width),
-        scales[:, :2, :kv_heads].astype(bf16),
+        scales.transpose(2, 0, 1),
     )
 
 

time: 107 us -> 103 us (0.963)
  local copies, waits for them, and re-layouts: 8.2 us -> 0 us
  Pallas kernels: 98.1 us -> 102 us
    unnamed x5 -> x0, local copies, waits for them, and re-layouts: 7.44 us -> none
    pallas_call x0 -> x1, Pallas kernels: none -> 3.55 us  [on_device(): pl.pallas_call(deliver, out_shape=(jax.ShapeDtypeStruct(proj.shape, bf16)...]
where the time goes in v2:
time: 103 us
  Pallas kernels  102 us (99%)
    pallas_call x1, Pallas kernels, on_device(): pl.pallas_call(functools.partial(kernel, groups, tps, capacity), out_shap...  98.4 us
    pallas_call x1, Pallas kernels, on_device(): pl.pallas_call(deliver, out_shape=(jax.ShapeDtypeStruct(proj.shape, bf16)...  3.55 us

profile of v2, /device:TPU:0, one launch (start us, length us, event | category | flops | bytes accessed | tf_op | source)
XLA Modules:
  0.0 102.6 jit_solution(10121169633832422123)
XLA Ops:
  0.6 98.4 %shard_map.121 = (bf16[512,1024]{1,0:T(8,128)(2,1)}, bf16[8,128,256]{2,1,0:T(8,128)(2,1)}, f32[8,8,128]{2,1,0:T(8,128)}) custom-call(bf16[8,64,2048]{2,1,0:T(8,128)(2,1)} %bitcast.8, bf16[8,64,256]{2,1,0:T(8,128)(2,1)} %bitcast.11, bf16[8,64,256]{2,1,0:T(8,128)(2,1)} %bitcast.12, bf16[16,64,256]{2,1,0:T(8,128)(2,1)} %pk_ref.1, bf16[16,64,256]{2,1,0:T(8,128)(2,1)} %pv_ref.1, ...), custom_call_target="tpu_custom_call" | custom-call | flops 11005853696 | bytes 16777216 | tf_op jit(solution)/shard_map/pallas_call | solution.py:372
  99.0 3.5 %shard_map.122 = (bf16[512,1024]{1,0:T(8,128)(2,1)}, bf16[8,128,256]{2,1,0:T(8,128)(2,1)}, bf16[2,2,8]{2,1,0:T(2,128)(2,1)}) custom-call(bf16[512,1024]{1,0:T(8,128)(2,1)} %get-tuple-element.9.proj_ref, bf16[8,128,256]{2,1,0:T(8,128)(2,1)} %get-tuple-element.10.page_ref, f32[8,8,128]{2,1,0:T(8,128)} %get-tuple-element.11.scale_ref), custom_call_target="tpu_custom_call" | custom-call | tf_op jit(solution)/shard_map/pallas_call | solution.py:415

commit v3 on v2

--- a/solution.py
+++ b/solution.py
@@ -10,7 +10,6 @@
 
 HEAD_SIZE = 128
 MESH = pl.DeviceIdType.MESH
-DEPTH = 2
 PIECES = 4
 
 
@@ -112,8 +111,9 @@
     far = last - me
 
     def dest_at(p):
-        right = p < far
-        return jnp.where(right, last - p, jnp.where(p < last, p - far, me))
+        rightward = jnp.where(p < far, last - p, p - far)
+        leftward = jnp.where(p < me, p, last - (p - me))
+        return jnp.where(p < last, jnp.where(2 * me > last, leftward, rightward), me)
 
     def w_copy(p):
         j = dest_at(p)
@@ -240,13 +240,6 @@
 
             @pl.when((p < last) & jnp.logical_not(has_upstream(j)))
             def _():
-                number = i * last + p
-
-                @pl.when(number >= DEPTH)
-                def _():
-                    before = number - DEPTH
-                    sum_copy(before // last, dest_at(before % last)).wait_send()
-
                 sum_copy(i, j).start()
 
             return carry
@@ -303,13 +296,13 @@
         def _():
             compute(i)
 
+        @pl.when(i > 1)
+        def _():
+            finish(i - 2)
+
         @pl.when(i > 0)
         def _():
             forward(i - 1)
-
-        @pl.when(i > 1)
-        def _():
-            finish(i - 2)
 
         return carry
 
@@ -319,10 +312,7 @@
 
     def drain(i, carry):
         def one(p, inner):
-            @pl.when(((me > 0) & (me < last)) | (i * last + p >= groups * last - DEPTH))
-            def _():
-                sum_copy(i, dest_at(p)).wait_send()
-
+            sum_copy(i, dest_at(p)).wait_send()
             return inner
 
         return lax.fori_loop(0, last, one, carry)

time: 103 us -> 85.6 us (0.83)
  Pallas kernels: 102 us -> 84.8 us
    pallas_call x1, Pallas kernels: 98.4 us -> 81.3 us  [on_device(): pl.pallas_call(functools.partial(kernel, groups, tps, capacity), out_shap...]
where the time goes in v3:
time: 85.6 us; the launch traced here: 85.5 us
  Pallas kernels  84.8 us (99%)
    pallas_call x1, Pallas kernels, on_device(): pl.pallas_call(functools.partial(kernel, groups, tps, capacity), out_shap...  81.3 us
    pallas_call x1, Pallas kernels, on_device(): pl.pallas_call(deliver, out_shape=(jax.ShapeDtypeStruct(proj.shape, bf16)...  3.55 us

profile of v3, /device:TPU:0, one launch (start us, length us, event | category | flops | bytes accessed | tf_op | source)
XLA Modules:
  0.0 85.5 jit_solution(6020399071055972166)
XLA Ops:
  0.6 81.3 %shard_map.121 = (bf16[512,1024]{1,0:T(8,128)(2,1)}, bf16[8,128,256]{2,1,0:T(8,128)(2,1)}, f32[8,8,128]{2,1,0:T(8,128)}) custom-call(bf16[8,64,2048]{2,1,0:T(8,128)(2,1)} %bitcast.8, bf16[8,64,256]{2,1,0:T(8,128)(2,1)} %bitcast.11, bf16[8,64,256]{2,1,0:T(8,128)(2,1)} %bitcast.12, bf16[16,64,256]{2,1,0:T(8,128)(2,1)} %pk_ref.1, bf16[16,64,256]{2,1,0:T(8,128)(2,1)} %pv_ref.1, ...), custom_call_target="tpu_custom_call" | custom-call | flops 11005853696 | bytes 16777216 | tf_op jit(solution)/shard_map/pallas_call | solution.py:362
  81.9 3.5 %shard_map.122 = (bf16[512,1024]{1,0:T(8,128)(2,1)}, bf16[8,128,256]{2,1,0:T(8,128)(2,1)}, bf16[2,2,8]{2,1,0:T(2,128)(2,1)}) custom-call(bf16[512,1024]{1,0:T(8,128)(2,1)} %get-tuple-element.9.proj_ref, bf16[8,128,256]{2,1,0:T(8,128)(2,1)} %get-tuple-element.10.page_ref, f32[8,8,128]{2,1,0:T(8,128)} %get-tuple-element.11.scale_ref), custom_call_target="tpu_custom_call" | custom-call | tf_op jit(solution)/shard_map/pallas_call | solution.py:405
